TPU v7x, 256 devices: a whole 4x4x8 slice. The times are simulated.
256 devices in a mesh: bx: 4 (over x), by: 4 (over y), vert: 16 (over z, core).
Axes of the slice: x: 4, y: 4, z: 8, core: 2. Of those that a mesh axis runs over, the one named last changes fastest.
Arguments:
- estimate: float32 [128, 128, 512], P('bx', 'by', 'vert'), may hold values from 0.5 to 1.5
- view_tiles: bfloat16 [4, 4, 16, 64, 64, 128], P('bx', 'by', 'vert'), may hold values from 0.19921875 to 2
- slot_view: int32 [4, 4, 4], P('bx', 'by'), may hold values from 0 to 3, each once within a row
- psf_taps: float32 [4, 3, 3, 33], replicated, may hold values from 0.05 to 1
Outputs:
- refined: float32 [128, 128, 512], P('bx', 'by', 'vert')
Inputs may be any that keep to these rules, and one draw needn't show every extreme that they name: `slot_view`: each block's list names every view once.
All inputs are finite; a program needn't handle non-finite values.
Results may differ from a plain program's by a relative error of at most 0.0003.
Values may be sent and summed in bfloat16 or wider, within the bound.
A program may use at most 128 MiB of HBM per device.

v0:
```python
import jax
import jax.numpy as jnp
from jax import lax
from jax.experimental import pallas as pl
from jax.experimental.pallas import tpu as pltpu
from jax.sharding import PartitionSpec as P

BACKGROUND = 0.1
MESH = pl.DeviceIdType.MESH
F32, BF16 = jnp.float32, jnp.bfloat16
BLOCK = 32
RAD = 16
TAPS = 33
RANK = 3
VIEWS = 4
GROUPS = 4
LANES = 128


def iota(shape, axis):
    return lax.broadcasted_iota(jnp.int32, shape, axis)


def dot(a, b):
    return jnp.dot(a, b, preferred_element_type=F32)


def band(line, rows, start):
    line = jnp.broadcast_to(line, (rows, LANES))
    return pltpu.roll(line, start % LANES, 1, stride=1, stride_axis=0)


def swap_quads(a, b):
    low, axis = iota(a.shape, a.ndim - 2) < 4, a.ndim - 2
    return jnp.where(low, a, pltpu.roll(b, 4, axis)), jnp.where(low, pltpu.roll(a, 4, axis), b)


def build_taps(psf, slot_view, slot, taps):
    listed = slot_view[...]
    view = jnp.sum(jnp.where(iota(listed.shape, 2) == slot, listed, 0), axis=2, keepdims=True)
    held = iota((VIEWS, TAPS), 0) == view[0]
    mine = jnp.sum(jnp.where(held[None, None], psf[...], 0.0), axis=2)
    mine = (mine / jnp.sum(mine, axis=-1, keepdims=True)).astype(BF16).astype(F32)
    taps[...] = jnp.zeros_like(taps)
    for a in range(3):
        taps[0, 8 * a : 8 * a + RANK, :TAPS] = mine[a]
    flip = (iota((LANES, LANES), 0) + iota((LANES, LANES), 1) == TAPS - 1).astype(BF16)
    taps[1] = dot(taps[0].astype(BF16), flip)


def build_z(taps, wz, wb):
    z_in, z_out = iota((LANES, LANES), 0), iota((LANES, LANES), 1)
    near = jnp.abs(z_in - z_out) <= RAD
    rim, out = iota((32, LANES), 0), iota((32, LANES), 1)
    rim_ok = ((rim < RAD) & (out <= rim)) | ((rim >= RAD) & (out >= rim + 96))
    lane16 = iota((16, LANES), 1)
    for r in range(RANK):
        forward, backward = taps[1, 16 + r : 17 + r, :], taps[0, 16 + r : 17 + r, :]
        columns = slice(r * LANES, (r + 1) * LANES)
        wz[0:128, columns] = jnp.where(near, band(forward, LANES, -RAD), 0.0).astype(BF16)
        wz[128:160, columns] = jnp.where(rim_ok, band(forward, 32, 96), 0.0).astype(BF16)
        wz[160:256, columns] = jnp.zeros((96, LANES), BF16)
        main = jnp.where(near, band(backward, LANES, -RAD), 0.0)
        low = jnp.where(lane16 < RAD, band(backward, 16, 0), 0.0)
        high = jnp.where(lane16 < RAD, band(backward, 16, 96), 0.0)
        for g in range(GROUPS):
            wb[g, r * 128 : r * 128 + 128, 0:128] = (
                pltpu.roll(main, 32 * g, 1) if g else main
            ).astype(BF16)
            wb[g, r * 128 : r * 128 + 128, 128:256] = jnp.zeros((128, LANES), BF16)
            lo, hi = pltpu.roll(low, RAD * g, 1) if g else low, pltpu.roll(high, 64 + RAD * g, 1)
            wb[g, r * 128 : r * 128 + 16, 128:256] = lo.astype(BF16)
            wb[g, r * 128 + 112 : r * 128 + 128, 128:256] = hi.astype(BF16)


def build_x(taps, bx, tx, txb):
    spread = (iota((LANES, 256), 1) == 4 * iota((LANES, 256), 0)).astype(BF16)
    lane, row = iota((LANES, LANES), 1), iota((LANES, LANES), 0)
    low, high = bx > 0, bx < 3

    def tiles(line):
        turned = [band(line[:, i * LANES : (i + 1) * LANES], LANES, 0) for i in range(2)]
        return jnp.where(lane >= row, turned[0], 0.0), jnp.where(lane >= row, turned[1], turned[0])

    wide = [dot(taps[k, 0:8, :].astype(BF16), spread) for k in range(2)]
    for r in range(RANK):
        left, right = tiles(wide[0][r : r + 1])
        tx[r, :, 0:128] = left.astype(BF16)
        tx[r, :, 128:256] = right.astype(BF16)
        left, right = [m[0:64] for m in tiles(wide[1][r : r + 1])]
        txb[0, r, :, 0:128] = jnp.where((lane[0:64] >= 64) | low, left, 0.0).astype(BF16)
        txb[0, r, :, 128:256] = right.astype(BF16)
        txb[1, r, :, 0:128] = left.astype(BF16)
        txb[1, r, :, 128:256] = jnp.where(high, right, 0.0).astype(BF16)


def build_y(taps, by, ty, tyb):
    place = by * BLOCK - RAD + iota((BLOCK, LANES), 1)
    inside = (place >= 0) & (place < 4 * BLOCK)
    plain = [band(taps[0, 8 + r : 9 + r, :], BLOCK, 0) for r in range(RANK)]
    plain += [
        jnp.where(inside, band(taps[1, 8 + r : 9 + r, :], BLOCK, 0), 0.0) for r in range(RANK)
    ]
    plain = jnp.concatenate(plain, axis=0).astype(BF16)
    y, column = iota((LANES, 256), 0), iota((LANES, 256), 1)
    wide = [
        dot(plain, (column == 16 * (y // 4) + 4 * x + y % 4).astype(BF16)).astype(BF16)
        for x in range(4)
    ]
    row, source = iota((LANES, LANES), 0), iota((LANES, LANES), 1)
    order = (row == 16 * (source % 32 // 4) + 4 * (source // 32) + source % 4).astype(BF16)
    for i in range(2 * RANK):
        done = dot(order, jnp.concatenate([m[i * 32 : i * 32 + 32] for m in wide], axis=0)).astype(BF16)
        if i < RANK:
            ty[i] = done
        else:
            tyb[(i - RANK) * 128 : (i - RANK + 1) * 128, :] = done


def kernel(
    est_hbm, tile_hbm, psf_hbm, slot_view_hbm, refined,
    est, tile, psf, slot_view,
    packed, parts, outer, field, after_z, after_x, seen, back_y, back_x, sums, rims,
    got_core, got_chip, got_edge,
    taps, tx, ty, wz, tyb, txb, wb,
    load_sem, part_send, part_recv, face_send, face_recv, core_send, core_recv, sum_send, sum_recv, ready,
):
    bx, by, vert = lax.axis_index("bx"), lax.axis_index("by"), lax.axis_index("vert")
    q, slot = vert // VIEWS, vert % VIEWS
    core, chip = slot % 2, slot // 2

    loads = [
        pltpu.make_async_copy(source, target, load_sem.at[i])
        for i, (source, target) in enumerate(
            ((est_hbm, est), (psf_hbm, psf), (slot_view_hbm, slot_view), (tile_hbm, tile))
        )
    ]
    for copy in loads:
        copy.start()

    def at_vert(index):
        return {"vert": index}

    partner = at_vert(q * 4 + chip * 2 + 1 - core)
    above, below = q < 3, q > 0
    first, last = slot == 0, slot == VIEWS - 1
    is_edge = (first & below) | (last & above)

    straight = core == 0

    def block(ju, jv):
        return jnp.where(straight, jv, ju), jnp.where(straight, ju, jv)

    def link(along_u, step):
        x_step = jnp.where(straight == along_u, step, 0)
        x, y = bx + x_step, by + step - x_step
        return {"bx": x, "by": y}, (x >= 0) & (x < 4) & (y >= 0) & (y < 4)

    u_up, u_down, v_up, v_down = link(True, 1), link(True, -1), link(False, 1), link(False, -1)

    def clear(ref):
        ref[...] = jnp.zeros(ref.shape, BF16)

    pl.when(bx == 0)(lambda: clear(field.at[:, 0, core]))
    pl.when(bx == 3)(lambda: clear(field.at[:, 2, core]))
    pl.when(by == 0)(lambda: clear(field.at[0, :, core]))
    pl.when(by == 3)(lambda: clear(field.at[2, :, core]))
    pl.when(~below)(lambda: clear(outer.at[0]))
    pl.when(~above)(lambda: clear(outer.at[1]))

    got_edge[...] = jnp.zeros_like(got_edge)
    barrier = pltpu.get_barrier_semaphore()

    def greet(device):
        pl.semaphore_signal(barrier, inc=1, device_id=device, device_id_type=MESH)

    for k in range(1, VIEWS):
        greet(at_vert(q * 4 + (slot + k) % VIEWS))
    for device, there in (u_up, u_down, v_up, v_down):
        pl.when(there)(lambda device=device: greet(device))

    @pl.when(above)
    def _():
        greet(at_vert(vert - slot + 4))

        @pl.when(last)
        def _():
            for k in range(2, VIEWS + 1):
                greet(at_vert(vert + k))

    loads[0].wait()
    groups = est[...].reshape(BLOCK, GROUPS, 8, BLOCK)
    line = jnp.concatenate([groups[:, g].reshape(256, BLOCK) for g in range(GROUPS)], axis=1)
    line = pltpu.roll(line, slot * 32, 1).reshape(16, 2, 8, LANES)
    for side, quads in enumerate(swap_quads(line[:, 0], line[:, 1])):
        packed[side * 128 : side * 128 + 128, :] = quads.reshape(128, LANES).astype(BF16)

    beside = [(there, 1) for _, there in (u_up, u_down, v_up, v_down)]
    beside += [(first & below, VIEWS), (~first & below, 1)]
    pl.semaphore_wait(barrier, 3 + sum(jnp.where(there, n, 0) for there, n in beside))

    def answer(device):
        pl.semaphore_signal(ready, inc=1, device_id=device, device_id_type=MESH)

    @pl.when(first & below)
    def _():
        for k in range(1, VIEWS + 1):
            answer(at_vert(vert - k))

    pl.when(~first & below)(lambda: answer(at_vert(vert - slot - 1)))

    def part_copy(source, send, device, side):
        return pltpu.make_async_remote_copy(
            src_ref=packed.at[pl.ds(side * 128, 128), :], dst_ref=parts.at[source],
            send_sem=part_send.at[send], recv_sem=part_recv.at[source],
            device_id=device, device_id_type=MESH,
        )

    for k in range(1, VIEWS):
        other = (slot + k) % VIEWS
        part_copy(slot, k - 1, at_vert(q * 4 + other), other % 2).start()

    def outer_copy(which, send, device, side):
        return pltpu.make_async_remote_copy(
            src_ref=packed.at[pl.ds(side * 128, 128), :], dst_ref=outer.at[which],
            send_sem=part_send.at[3 + send], recv_sem=part_recv.at[4 + which],
            device_id=device, device_id_type=MESH,
        )

    @pl.when(first & below)
    def _():
        for k in range(VIEWS):
            outer_copy(1, k, at_vert(vert - 4 + k), k % 2).start()

    parts[slot] = packed[pl.ds(core * 128, 128), :]
    loads[1].wait()
    loads[2].wait()
    build_taps(psf, slot_view, slot, taps)
    build_z(taps, wz, wb)

    def assemble():
        for k in range(1, VIEWS):
            part_copy((slot + k) % VIEWS, 0, partner, 0).wait_recv()
        chunk = iota((128, LANES), 1) // 32
        have = [parts[k].astype(F32) for k in range(VIEWS)]
        for g in range(GROUPS):
            line = have[(3 - g) % 4]
            for at in range(3):
                line = jnp.where(chunk == at, have[(at - g) % 4], line)
            if g:
                line = pltpu.roll(line, LANES - 32 * g, 1)
            for tp in range(2):
                field[1, 1, core, 6 * tp + g] = line[64 * tp : 64 * tp + 64].astype(BF16)

    def assemble_rims():
        for k, there in enumerate((below, above)):
            pl.when(there)(lambda k=k: outer_copy(k, 0, partner, 0).wait_recv())
        is_above = iota((128, LANES), 1) % 32 < RAD
        line = jnp.where(is_above, outer[1].astype(F32), outer[0].astype(F32))
        field[1, 1, core, 4:6] = pltpu.roll(line, RAD, 1).astype(BF16).reshape(2, 64, LANES)

    def message(ju, jv, which):
        return field.at[(*block(ju, jv), core, slice(4, 10) if which else slice(0, 4))]

    def face_copy(source, target, which, send, device):
        return pltpu.make_async_remote_copy(
            src_ref=message(*source, which), dst_ref=message(*target, which),
            send_sem=face_send.at[send],
            recv_sem=face_recv.at[which * 9 + target[0] * 3 + target[1]],
            device_id=device, device_id_type=MESH,
        )

    ways = {"u_up": (0, u_up, (0, 1)), "u_down": (1, u_down, (2, 1)), "v_up": (2, v_up, (1, 0)), "v_down": (3, v_down, (1, 2))}

    def send_own(name, which):
        index, (device, there), target = ways[name]
        pl.when(there)(face_copy((1, 1), target, which, index, device).start)

    def relay(name, along, which):
        index, (device, there), target = ways[name]
        source = (along, 1) if name[0] == "v" else (1, along)
        target = (along, target[1]) if name[0] == "v" else (target[0], along)
        pl.when(there)(face_copy(source, target, which, 4 + index, device).start)

    def came(ju, jv, which, over):
        there = ways[f"{over}_{'down' if (jv if over == 'v' else ju) == 0 else 'up'}"][1][1]
        copy = face_copy((ju, jv), (ju, jv), which, 0, partner)
        pl.when(there)(copy.wait_recv)

    def core_copy(jy, jx, side):
        return pltpu.make_async_remote_copy(
            src_ref=field.at[jy, jx, side], dst_ref=field.at[jy, jx, side],
            send_sem=core_send.at[0], recv_sem=core_recv.at[jy * 3 + jx],
            device_id=partner, device_id_type=MESH,
        )

    def pass_on(ju, jv):
        core_copy(*block(ju, jv), core).start()

    def swapped(jy, jx):
        core_copy(jy, jx, 1 - core).wait_recv()

    def forward_z(jy, jx):
        rows = slice(jx * 128, jx * 128 + 128)
        rim = field[jy, jx, :, 4:6].reshape(256, LANES)
        for g in range(GROUPS):
            turned = pltpu.roll(rim, LANES - 32 * g, 1) if g else rim
            main = jnp.concatenate(
                [field[jy, jx, side, 6 * tp + g] for side in range(2) for tp in range(2)], axis=0
            )
            done = dot(jnp.concatenate([main, turned], axis=1), wz[...]).astype(BF16)
            for r in range(RANK):
                after_z[r, jy * GROUPS + g, :, rows, :] = done[:, r * 128 : (r + 1) * 128].reshape(
                    2, 128, LANES
                )

    def forward_x(jy):
        for r in range(RANK):
            for group in (jy * GROUPS, jy * GROUPS + 2):
                for b in range(2):
                    rows = slice(b * 128, b * 128 + 256)
                    both = [after_z[r, group + k // 2, k % 2, rows, :] for k in range(4)]
                    done = dot(tx[r], jnp.concatenate(both, axis=1)).astype(BF16)
                    for k in range(4):
                        after_x[r, group + k // 2, k % 2, b * 128 : b * 128 + 128, :] = done[
                            :, k * 128 : k * 128 + 128
                        ]

    assemble()
    for name in ("u_up", "u_down", "v_up", "v_down"):
        send_own(name, 0)

    @pl.when(last & above)
    def _():
        pl.semaphore_wait(ready, VIEWS)
        for k in range(VIEWS):
            outer_copy(0, k, at_vert(vert + 1 + k), k % 2).start()

    assemble_rims()
    for name in ("v_up", "v_down", "u_up", "u_down"):
        send_own(name, 1)
    pass_on(1, 1)
    build_x(taps, bx, tx, txb)
    for side in (0, 2):
        came(side, 1, 0, "u")
    for one, other in ((0, 2), (2, 0)):
        relay("v_up", one, 0)
        relay("v_down", other, 0)
    for side in (0, 2):
        came(1, side, 1, "v")
    for one, other in ((0, 2), (2, 0)):
        relay("u_up", one, 1)
        relay("u_down", other, 1)
    build_y(taps, by, ty, tyb)
    loads[3].wait()

    def order_tile(i, carry):
        quad = tile[pl.ds(4 * i, 4)].astype(F32).reshape(2, 2, 8, 8, LANES)
        sides = swap_quads(quad[:, 0], quad[:, 1])
        rows = jnp.stack([m[x] for m in sides for x in range(2)], axis=1)
        seen[i] = rows.reshape(256, LANES).astype(BF16)
        return carry

    lax.fori_loop(0, 16, order_tile, 0, unroll=4)
    swapped(1, 1)
    forward_z(1, 1)
    for side in (0, 2):
        came(side, 1, 1, "u")
        pass_on(side, 1)
        came(1, side, 0, "v")
        pass_on(1, side)
    for side in (0, 2):
        swapped(1, side)
        swapped(side, 1)
    for side in (0, 2):
        forward_z(1, side)
        forward_z(side, 1)
    waves = (((0, 0), (2, 2)), ((0, 2), (2, 0)))
    for corner in waves[0]:
        came(*corner, 0, "v")
        came(*corner, 1, "u")
        pass_on(*corner)
    forward_x(1)
    for corner in waves[1]:
        came(*corner, 0, "v")
        came(*corner, 1, "u")
        pass_on(*corner)
    for wave in waves:
        for corner in wave:
            swapped(*corner)
        for corner in wave:
            forward_z(*corner)
    for jy in (0, 2):
        forward_x(jy)

    def along_y(step):
        quotient = []
        for b in range(2):
            blurred = None
            for r in range(RANK):
                quads = [
                    after_x[r, 4 * b : 4 * b + 8, :, 16 * i : 16 * i + 16, :].reshape(256, LANES)
                    for i in range(4 * step, 4 * step + 4)
                ]
                part = dot(ty[r], jnp.concatenate(quads, axis=1))
                blurred = part if blurred is None else blurred + part
            rows = slice(128 * b, 128 * b + 128)
            quads = [seen[i, rows, :] for i in range(4 * step, 4 * step + 4)]
            quads = jnp.concatenate(quads, axis=1).astype(F32)
            quotient.append((RANK * quads / (blurred + RANK * BACKGROUND)).astype(BF16))
        quotient = jnp.concatenate(quotient, axis=0)
        for r in range(RANK):
            done = dot(tyb[r * 128 : r * 128 + 128, :], quotient).astype(BF16)
            for k in range(4):
                i = 4 * step + k
                back_y[r * 8 : r * 8 + 8, 16 * i : 16 * i + 16, :] = done[
                    :, k * 128 : k * 128 + 128
                ].reshape(8, 16, LANES)

    def backward_x(half):
        within = slice(half * 64, half * 64 + 192)
        for g in (0, 2):
            for r in range(RANK):
                at = (r * GROUPS + g) * 2
                sides = jnp.concatenate([back_y[at + k, within, :] for k in range(4)], axis=1)
                done = dot(txb[half, r, :, 0:192], sides).astype(BF16)
                for k in range(4):
                    rows = slice(k % 2 * 64, k % 2 * 64 + 64)
                    back_x[g + k // 2, half, rows, r * 128 : (r + 1) * 128] = done[
                        :, k * 128 : k * 128 + 128
                    ]

    def backward_z(half):
        parts_z = [dot(back_x[g, half], wb[g]) for g in range(GROUPS)]
        both = (parts_z[0] + parts_z[1] + (parts_z[2] + parts_z[3]))[:, LANES:]
        is_low = iota((64, LANES), 1) < 64
        rims[half, 0] = jnp.where(is_low, both[0:64], pltpu.roll(both[64:128], 64, 1))
        rims[half, 1] = jnp.where(is_low, pltpu.roll(both[0:64], 64, 1), both[64:128])
        for which in range(2):
            pl.when((below, above)[which])(rim_copy(half, which).start)
        for g in range(GROUPS):
            for c in range(4):
                at = (g + c) % 4
                sums[half, c, :, at * 32 : at * 32 + 32] = parts_z[g][:, at * 32 : at * 32 + 32]

    far = (1 - chip) * 2 + core

    def sum_copy(source, target, index, device):
        return pltpu.make_async_remote_copy(
            src_ref=source, dst_ref=target, send_sem=sum_send.at[index],
            recv_sem=sum_recv.at[index], device_id=device, device_id_type=MESH,
        )

    far_swap = [
        sum_copy(sums.at[h, (1 - chip) * 2 + 1 - core], got_core.at[h, 0], h, partner) for h in range(2)
    ]
    near_swap = [
        sum_copy(sums.at[h, chip * 2 + 1 - core], got_core.at[h, 1], 2 + h, partner) for h in range(2)
    ]
    over = [sum_copy(sums.at[h, far], got_chip.at[h], 4 + h, at_vert(q * 4 + far)) for h in range(2)]

    def rim_copy(h, which):
        home = (vert - slot - 1, vert - slot + 4)[which]
        return pltpu.make_async_remote_copy(
            src_ref=rims.at[h, which], dst_ref=got_edge.at[slot, h], send_sem=sum_send.at[6 + 2 * h + which],
            recv_sem=sum_recv.at[6 + 2 * slot + h], device_id=at_vert(home), device_id_type=MESH,
        )

    def rim_came(h):
        for k in range(VIEWS):
            pltpu.make_async_remote_copy(
                src_ref=rims.at[h, 0], dst_ref=got_edge.at[k, h], send_sem=sum_send.at[6],
                recv_sem=sum_recv.at[6 + 2 * k + h], device_id=partner, device_id_type=MESH,
            ).wait_recv()

    def backward(h):
        backward_x(h)
        backward_z(h)
        far_swap[h].start()
        near_swap[h].start()

    def pass_over(h):
        far_swap[h].wait_recv()
        sums[h, far] = sums[h, far] + got_core[h, 0]
        over[h].start()

    pl.when(~last & above)(lambda: pl.semaphore_wait(ready, 1))
    for step in range(3):
        along_y(step)
    backward(0)
    along_y(3)
    pass_over(0)
    backward(1)
    pass_over(1)

    for k in range(1, VIEWS):
        part_copy(slot, k - 1, partner, 0).wait_send()

    @pl.when(is_edge)
    def _():
        for k in range(VIEWS):
            outer_copy(0, k, partner, 0).wait_send()

    def sent(ref, semaphore):
        pltpu.make_async_remote_copy(
            src_ref=ref, dst_ref=ref, send_sem=semaphore, recv_sem=face_recv.at[0],
            device_id=partner, device_id_type=MESH,
        ).wait_send()

    for name, (index, (_, there), _) in ways.items():
        relayed = field.at[0:2, 0:2, :, 0:1] if name[0] == "v" else field.at[0:3, 0:2, :, 0:1]

        @pl.when(there)
        def _():
            sent(field.at[1, 1, core], face_send.at[index])
            sent(relayed, face_send.at[4 + index])

    sent(field.at[:, :, core], core_send.at[0])

    start = jnp.where(last, RAD, 0)
    lane = iota((64, LANES), 1)
    keep = is_edge & (lane >= start) & (lane < start + RAD)
    for h in range(2):
        near_swap[h].wait_recv()
        mine = sums[h, slot] + got_core[h, 1]
        over[h].wait_recv()
        mine = mine + got_chip[h]

        pl.when(is_edge)(lambda: rim_came(h))
        edge = got_edge[0, h] + got_edge[1, h] + (got_edge[2, h] + got_edge[3, h])
        for g in range(GROUPS):
            own = pltpu.roll(mine, (8 - g - slot) % 4 * 32, 1)
            sides = []
            for k in range(2):
                rim = pltpu.roll(edge, (start + LANES - 64 * k - RAD * g) % LANES, 1)
                part = own[64 * k : 64 * k + 64] + jnp.where(keep, rim, 0.0)
                sides.append(part.reshape(8, 8, LANES) * (1.0 / (RANK * VIEWS)))
            part = jnp.stack(swap_quads(*sides), axis=1).reshape(16, 8, LANES)
            at = (slice(16 * h, 16 * h + 16), slice(g * 8, g * 8 + 8))
            refined[at] = est[at] * part[:, :, 0:BLOCK]

    for copy in far_swap + near_swap + over:
        copy.wait_send()
    for which in range(2):

        @pl.when((below, above)[which])
        def _():
            for h in range(2):
                rim_copy(h, which).wait_send()


def local(estimate, view_tiles, slot_view, psf_taps):
    vmem = pl.BlockSpec(memory_space=pltpu.VMEM)
    hbm = pl.BlockSpec(memory_space=pltpu.HBM)
    tile = view_tiles[0, 0, 0]
    psf = jnp.transpose(psf_taps, (1, 2, 0, 3))
    scratch = [
        pltpu.VMEM(estimate.shape, F32),
        pltpu.VMEM(tile.shape, BF16),
        pltpu.VMEM(psf.shape, F32),
        pltpu.VMEM(slot_view.shape, jnp.int32),
        pltpu.VMEM((256, LANES), BF16),
        pltpu.VMEM((VIEWS, 128, LANES), BF16),
        pltpu.VMEM((2, 128, LANES), BF16),
        pltpu.VMEM((3, 3, 2, 10, 64, LANES), BF16),
        pltpu.VMEM((RANK, 12, 2, 384, LANES), BF16),
        pltpu.VMEM((RANK, 12, 2, 256, LANES), BF16),
        pltpu.VMEM((16, 256, LANES), BF16),
        pltpu.VMEM((24, 256, LANES), BF16),
        pltpu.VMEM((GROUPS, 2, 128, RANK * LANES), BF16),
        pltpu.VMEM((2, 4, 128, LANES), F32),
        pltpu.VMEM((2, 2, 64, LANES), F32),
        pltpu.VMEM((2, 2, 128, LANES), F32),
        pltpu.VMEM((2, 128, LANES), F32),
        pltpu.VMEM((VIEWS, 2, 64, LANES), F32),
        pltpu.VMEM((2, 24, LANES), F32),
        pltpu.VMEM((RANK, 128, 256), BF16),
        pltpu.VMEM((RANK, 128, 256), BF16),
        pltpu.VMEM((256, RANK * LANES), BF16),
        pltpu.VMEM((RANK * 128, 256), BF16),
        pltpu.VMEM((2, RANK, 64, 256), BF16),
        pltpu.VMEM((GROUPS, RANK * LANES, 256), BF16),
        pltpu.SemaphoreType.DMA((4,)),
        pltpu.SemaphoreType.DMA((7,)),
        pltpu.SemaphoreType.DMA((6,)),
        pltpu.SemaphoreType.DMA((8,)),
        pltpu.SemaphoreType.DMA((18,)),
        pltpu.SemaphoreType.DMA((1,)),
        pltpu.SemaphoreType.DMA((9,)),
        pltpu.SemaphoreType.DMA((10,)),
        pltpu.SemaphoreType.DMA((14,)),
        pltpu.SemaphoreType.REGULAR,
    ]
    return pl.pallas_call(
        kernel,
        out_shape=pltpu.VMEM(estimate.shape, F32),
        in_specs=[hbm] * 4,
        out_specs=vmem,
        scratch_shapes=scratch,
        compiler_params=pltpu.CompilerParams(
            collective_id=0, has_side_effects=True, vmem_limit_bytes=56 * 1024 * 1024
        ),
    )(*(pltpu.with_memory_space_constraint(a, pltpu.HBM) for a in (estimate, tile, psf, slot_view)))


def solution(mesh):
    placed = (
        P("bx", "by", "vert"),
        P("bx", "by", "vert", None, None, None),
        P("bx", "by", None),
        P(),
    )
    return jax.shard_map(
        local, mesh=mesh, in_specs=placed, out_specs=P("bx", "by", "vert"), check_vma=False
    )
```

profile of v0, /device:TPU:99, one launch (start us, length us, event | category | flops | bytes accessed | tf_op | source)
XLA Modules:
  0.0 32.5 jit_solution(1597425984070608798)
XLA Ops:
  0.0 31.7 %shard_map.46 = f32[32,32,32]{2,1,0:T(8,128)S(1)} custom-call(f32[32,32,32]{2,1,0:T(8,128)} %est_hbm.1, bf16[64,64,128]{2,1,0:T(8,128)(2,1)} %bitcast.2, f32[3,3,4,33]{3,2,1,0:T(4,128)} %bitcast.3, s32[1,1,4]{2,1,0:T(1,128)} %slot_view_hbm.1), custom_call_target="tpu_custom_call" | custom-call | tf_op jit(solution)/shard_map/pallas_call | solution.py:594
  31.7 0.8 %copy.6 = f32[32,32,32]{2,1,0:T(8,128)} copy(f32[32,32,32]{2,1,0:T(8,128)S(1)} %shard_map.46) | data formatting | bytes 262144
where the time goes:
time: 32.6 us; the launch traced here: 32.5 us
  Pallas kernels  31.7 us (97%)
  local copies, waits for them, and re-layouts  0.8 us (2%)
    pallas_call x1, Pallas kernels, local(): pl.pallas_call(kernel, out_shape=pltpu.VMEM(estimate.shape, F32), in_spec...  31.7 us
    unnamed x1, local copies, waits for them, and re-layouts  0.8 us

commit v1 on v0

--- a/solution.py
+++ b/solution.py
@@ -188,26 +188,26 @@
             for k in range(2, VIEWS + 1):
                 greet(at_vert(vert + k))
 
+    beside = [(there, 1) for _, there in (u_up, u_down, v_up, v_down)]
+    beside += [(first & below, VIEWS), (~first & below, 1)]
+    pl.semaphore_wait(barrier, 3 + sum(jnp.where(there, n, 0) for there, n in beside))
+
+    def answer(device):
+        pl.semaphore_signal(ready, inc=1, device_id=device, device_id_type=MESH)
+
+    @pl.when(first & below)
+    def _():
+        for k in range(1, VIEWS + 1):
+            answer(at_vert(vert - k))
+
+    pl.when(~first & below)(lambda: answer(at_vert(vert - slot - 1)))
+
     loads[0].wait()
     groups = est[...].reshape(BLOCK, GROUPS, 8, BLOCK)
     line = jnp.concatenate([groups[:, g].reshape(256, BLOCK) for g in range(GROUPS)], axis=1)
     line = pltpu.roll(line, slot * 32, 1).reshape(16, 2, 8, LANES)
     for side, quads in enumerate(swap_quads(line[:, 0], line[:, 1])):
         packed[side * 128 : side * 128 + 128, :] = quads.reshape(128, LANES).astype(BF16)
-
-    beside = [(there, 1) for _, there in (u_up, u_down, v_up, v_down)]
-    beside += [(first & below, VIEWS), (~first & below, 1)]
-    pl.semaphore_wait(barrier, 3 + sum(jnp.where(there, n, 0) for there, n in beside))
-
-    def answer(device):
-        pl.semaphore_signal(ready, inc=1, device_id=device, device_id_type=MESH)
-
-    @pl.when(first & below)
-    def _():
-        for k in range(1, VIEWS + 1):
-            answer(at_vert(vert - k))
-
-    pl.when(~first & below)(lambda: answer(at_vert(vert - slot - 1)))
 
     def part_copy(source, send, device, side):
         return pltpu.make_async_remote_copy(
@@ -250,17 +250,17 @@
             if g:
                 line = pltpu.roll(line, LANES - 32 * g, 1)
             for tp in range(2):
-                field[1, 1, core, 6 * tp + g] = line[64 * tp : 64 * tp + 64].astype(BF16)
+                field[1, 1, core, 4 * tp + g] = line[64 * tp : 64 * tp + 64].astype(BF16)
 
     def assemble_rims():
         for k, there in enumerate((below, above)):
             pl.when(there)(lambda k=k: outer_copy(k, 0, partner, 0).wait_recv())
         is_above = iota((128, LANES), 1) % 32 < RAD
         line = jnp.where(is_above, outer[1].astype(F32), outer[0].astype(F32))
-        field[1, 1, core, 4:6] = pltpu.roll(line, RAD, 1).astype(BF16).reshape(2, 64, LANES)
+        field[1, 1, core, 8:10] = pltpu.roll(line, RAD, 1).astype(BF16).reshape(2, 64, LANES)
 
     def message(ju, jv, which):
-        return field.at[(*block(ju, jv), core, slice(4, 10) if which else slice(0, 4))]
+        return field.at[(*block(ju, jv), core, slice(4 * which, min(4 * which + 4, 10)))]
 
     def face_copy(source, target, which, send, device):
         return pltpu.make_async_remote_copy(
@@ -302,11 +302,11 @@
 
     def forward_z(jy, jx):
         rows = slice(jx * 128, jx * 128 + 128)
-        rim = field[jy, jx, :, 4:6].reshape(256, LANES)
+        rim = field[jy, jx, :, 8:10].reshape(256, LANES)
         for g in range(GROUPS):
             turned = pltpu.roll(rim, LANES - 32 * g, 1) if g else rim
             main = jnp.concatenate(
-                [field[jy, jx, side, 6 * tp + g] for side in range(2) for tp in range(2)], axis=0
+                [field[jy, jx, side, 4 * tp + g] for side in range(2) for tp in range(2)], axis=0
             )
             done = dot(jnp.concatenate([main, turned], axis=1), wz[...]).astype(BF16)
             for r in range(RANK):
@@ -329,6 +329,8 @@
     assemble()
     for name in ("u_up", "u_down", "v_up", "v_down"):
         send_own(name, 0)
+    for name in ("v_up", "v_down", "u_up", "u_down"):
+        send_own(name, 1)
 
     @pl.when(last & above)
     def _():
@@ -336,11 +338,11 @@
         for k in range(VIEWS):
             outer_copy(0, k, at_vert(vert + 1 + k), k % 2).start()
 
+    build_x(taps, bx, tx, txb)
     assemble_rims()
-    for name in ("v_up", "v_down", "u_up", "u_down"):
-        send_own(name, 1)
+    for name in ("u_up", "u_down", "v_up", "v_down"):
+        send_own(name, 2)
     pass_on(1, 1)
-    build_x(taps, bx, tx, txb)
     for side in (0, 2):
         came(side, 1, 0, "u")
     for one, other in ((0, 2), (2, 0)):
@@ -351,6 +353,11 @@
     for one, other in ((0, 2), (2, 0)):
         relay("u_up", one, 1)
         relay("u_down", other, 1)
+    for side in (0, 2):
+        came(side, 1, 2, "u")
+    for one, other in ((0, 2), (2, 0)):
+        relay("v_up", one, 2)
+        relay("v_down", other, 2)
     build_y(taps, by, ty, tyb)
     loads[3].wait()
 
@@ -368,6 +375,7 @@
         came(side, 1, 1, "u")
         pass_on(side, 1)
         came(1, side, 0, "v")
+        came(1, side, 2, "v")
         pass_on(1, side)
     for side in (0, 2):
         swapped(1, side)
@@ -379,11 +387,13 @@
     for corner in waves[0]:
         came(*corner, 0, "v")
         came(*corner, 1, "u")
+        came(*corner, 2, "v")
         pass_on(*corner)
     forward_x(1)
     for corner in waves[1]:
         came(*corner, 0, "v")
         came(*corner, 1, "u")
+        came(*corner, 2, "v")
         pass_on(*corner)
     for wave in waves:
         for corner in wave:
@@ -508,7 +518,7 @@
         ).wait_send()
 
     for name, (index, (_, there), _) in ways.items():
-        relayed = field.at[0:2, 0:2, :, 0:1] if name[0] == "v" else field.at[0:3, 0:2, :, 0:1]
+        relayed = field.at[0:3, 0:2, :, 0:1] if name[0] == "v" else field.at[0:2, 0:2, :, 0:1]
 
         @pl.when(there)
         def _():
@@ -584,7 +594,7 @@
         pltpu.SemaphoreType.DMA((7,)),
         pltpu.SemaphoreType.DMA((6,)),
         pltpu.SemaphoreType.DMA((8,)),
-        pltpu.SemaphoreType.DMA((18,)),
+        pltpu.SemaphoreType.DMA((27,)),
         pltpu.SemaphoreType.DMA((1,)),
         pltpu.SemaphoreType.DMA((9,)),
         pltpu.SemaphoreType.DMA((10,)),

time: 32.6 us -> 31.5 us (0.966)
  Pallas kernels: 31.7 us -> 30.6 us
    pallas_call x1, Pallas kernels: 31.7 us -> 30.6 us  [local(): pl.pallas_call(kernel, out_shape=pltpu.VMEM(estimate.shape, F32), in_spec...]
where the time goes in v1:
time: 31.5 us; the launch traced here: 31.4 us
  Pallas kernels  30.6 us (97%)
  local copies, waits for them, and re-layouts  0.8 us (3%)
    pallas_call x1, Pallas kernels, local(): pl.pallas_call(kernel, out_shape=pltpu.VMEM(estimate.shape, F32), in_spec...  30.6 us
    unnamed x1, local copies, waits for them, and re-layouts  0.8 us

profile of v1, /device:TPU:99, one launch (start us, length us, event | category | flops | bytes accessed | tf_op | source)
XLA Modules:
  0.0 31.4 jit_solution(10129651182657551725)
XLA Ops:
  0.0 30.6 %shard_map.46 = f32[32,32,32]{2,1,0:T(8,128)S(1)} custom-call(f32[32,32,32]{2,1,0:T(8,128)} %est_hbm.1, bf16[64,64,128]{2,1,0:T(8,128)(2,1)} %bitcast.2, f32[3,3,4,33]{3,2,1,0:T(4,128)} %bitcast.3, s32[1,1,4]{2,1,0:T(1,128)} %slot_view_hbm.1), custom_call_target="tpu_custom_call" | custom-call | tf_op jit(solution)/shard_map/pallas_call | solution.py:604
  30.6 0.8 %copy.6 = f32[32,32,32]{2,1,0:T(8,128)} copy(f32[32,32,32]{2,1,0:T(8,128)S(1)} %shard_map.46) | data formatting | bytes 262144

commit v2 on v1

--- a/solution.py
+++ b/solution.py
@@ -348,17 +348,12 @@
     for one, other in ((0, 2), (2, 0)):
         relay("v_up", one, 0)
         relay("v_down", other, 0)
+    build_y(taps, by, ty, tyb)
     for side in (0, 2):
         came(1, side, 1, "v")
     for one, other in ((0, 2), (2, 0)):
         relay("u_up", one, 1)
         relay("u_down", other, 1)
-    for side in (0, 2):
-        came(side, 1, 2, "u")
-    for one, other in ((0, 2), (2, 0)):
-        relay("v_up", one, 2)
-        relay("v_down", other, 2)
-    build_y(taps, by, ty, tyb)
     loads[3].wait()
 
     def order_tile(i, carry):
@@ -371,6 +366,11 @@
     lax.fori_loop(0, 16, order_tile, 0, unroll=4)
     swapped(1, 1)
     forward_z(1, 1)
+    for side in (0, 2):
+        came(side, 1, 2, "u")
+    for one, other in ((0, 2), (2, 0)):
+        relay("v_up", one, 2)
+        relay("v_down", other, 2)
     for side in (0, 2):
         came(side, 1, 1, "u")
         pass_on(side, 1)

time: 31.5 us -> 30.7 us (0.975)
  Pallas kernels: 30.6 us -> 29.5 us
    pallas_call x1, Pallas kernels: 30.6 us -> 29.5 us  [local(): pl.pallas_call(kernel, out_shape=pltpu.VMEM(estimate.shape, F32), in_spec...]
where the time goes in v2:
time: 30.7 us; the launch traced here: 30.3 us
  Pallas kernels  29.5 us (96%)
  local copies, waits for them, and re-layouts  0.8 us (3%)
    pallas_call x1, Pallas kernels, local(): pl.pallas_call(kernel, out_shape=pltpu.VMEM(estimate.shape, F32), in_spec...  29.5 us
    unnamed x1, local copies, waits for them, and re-layouts  0.8 us

profile of v2, /device:TPU:99, one launch (start us, length us, event | category | flops | bytes accessed | tf_op | source)
XLA Modules:
  0.0 30.3 jit_solution(4005142740563624638)
XLA Ops:
  0.0 29.5 %shard_map.46 = f32[32,32,32]{2,1,0:T(8,128)S(1)} custom-call(f32[32,32,32]{2,1,0:T(8,128)} %est_hbm.1, bf16[64,64,128]{2,1,0:T(8,128)(2,1)} %bitcast.2, f32[3,3,4,33]{3,2,1,0:T(4,128)} %bitcast.3, s32[1,1,4]{2,1,0:T(1,128)} %slot_view_hbm.1), custom_call_target="tpu_custom_call" | custom-call | tf_op jit(solution)/shard_map/pallas_call | solution.py:604
  29.6 0.8 %copy.6 = f32[32,32,32]{2,1,0:T(8,128)} copy(f32[32,32,32]{2,1,0:T(8,128)S(1)} %shard_map.46) | data formatting | bytes 262144

commit v3 on v2

--- a/solution.py
+++ b/solution.py
@@ -300,19 +300,19 @@
     def swapped(jy, jx):
         core_copy(jy, jx, 1 - core).wait_recv()
 
-    def forward_z(jy, jx):
-        rows = slice(jx * 128, jx * 128 + 128)
-        rim = field[jy, jx, :, 8:10].reshape(256, LANES)
+    def forward_z(*pieces):
+        rim = jnp.concatenate([field[jy, jx, side, 8 + tp] for jy, jx, side in pieces for tp in range(2)])
         for g in range(GROUPS):
             turned = pltpu.roll(rim, LANES - 32 * g, 1) if g else rim
             main = jnp.concatenate(
-                [field[jy, jx, side, 4 * tp + g] for side in range(2) for tp in range(2)], axis=0
+                [field[jy, jx, side, 4 * tp + g] for jy, jx, side in pieces for tp in range(2)]
             )
             done = dot(jnp.concatenate([main, turned], axis=1), wz[...]).astype(BF16)
-            for r in range(RANK):
-                after_z[r, jy * GROUPS + g, :, rows, :] = done[:, r * 128 : (r + 1) * 128].reshape(
-                    2, 128, LANES
-                )
+            for i, (jy, jx, side) in enumerate(pieces):
+                for r in range(RANK):
+                    after_z[r, jy * GROUPS + g, side, jx * 128 : jx * 128 + 128, :] = done[
+                        i * 128 : (i + 1) * 128, r * 128 : (r + 1) * 128
+                    ]
 
     def forward_x(jy):
         for r in range(RANK):
@@ -365,7 +365,7 @@
 
     lax.fori_loop(0, 16, order_tile, 0, unroll=4)
     swapped(1, 1)
-    forward_z(1, 1)
+    forward_z((1, 1, 0), (1, 1, 1))
     for side in (0, 2):
         came(side, 1, 2, "u")
     for one, other in ((0, 2), (2, 0)):
@@ -377,29 +377,33 @@
         came(1, side, 0, "v")
         came(1, side, 2, "v")
         pass_on(1, side)
-    for side in (0, 2):
-        swapped(1, side)
-        swapped(side, 1)
-    for side in (0, 2):
-        forward_z(1, side)
-        forward_z(side, 1)
+    face_pairs = (((1, 0), (1, 2)), ((0, 1), (2, 1)))
     waves = (((0, 0), (2, 2)), ((0, 2), (2, 0)))
-    for corner in waves[0]:
-        came(*corner, 0, "v")
-        came(*corner, 1, "u")
-        came(*corner, 2, "v")
-        pass_on(*corner)
+
+    def wave_came(wave):
+        for corner in wave:
+            came(*corner, 0, "v")
+            came(*corner, 1, "u")
+            came(*corner, 2, "v")
+            pass_on(*corner)
+
+    for one, other in face_pairs:
+        forward_z((*one, core), (*other, core))
+    for one, other in face_pairs:
+        swapped(*one)
+        swapped(*other)
+    for one, other in face_pairs:
+        forward_z((*one, 1 - core), (*other, 1 - core))
+    wave_came(waves[0])
     forward_x(1)
-    for corner in waves[1]:
-        came(*corner, 0, "v")
-        came(*corner, 1, "u")
-        came(*corner, 2, "v")
-        pass_on(*corner)
-    for wave in waves:
-        for corner in wave:
-            swapped(*corner)
-        for corner in wave:
-            forward_z(*corner)
+    wave_came(waves[1])
+    for one, other in waves:
+        forward_z((*one, core), (*other, core))
+    for one, other in waves:
+        swapped(*one)
+        swapped(*other)
+    for one, other in waves:
+        forward_z((*one, 1 - core), (*other, 1 - core))
     for jy in (0, 2):
         forward_x(jy)
 

time: 30.7 us -> 30.9 us (level)
  no operation moved by 1% of the time
where the time goes in v3:
time: 30.9 us; the launch traced here: 30.6 us
  Pallas kernels  29.8 us (96%)
  local copies, waits for them, and re-layouts  0.8 us (3%)
    pallas_call x1, Pallas kernels, local(): pl.pallas_call(kernel, out_shape=pltpu.VMEM(estimate.shape, F32), in_spec...  29.8 us
    unnamed x1, local copies, waits for them, and re-layouts  0.8 us

profile of v3, /device:TPU:99, one launch (start us, length us, event | category | flops | bytes accessed | tf_op | source)
XLA Modules:
  0.0 30.6 jit_solution(13993557731987488284)
XLA Ops:
  0.0 29.8 %shard_map.46 = f32[32,32,32]{2,1,0:T(8,128)S(1)} custom-call(f32[32,32,32]{2,1,0:T(8,128)} %est_hbm.1, bf16[64,64,128]{2,1,0:T(8,128)(2,1)} %bitcast.2, f32[3,3,4,33]{3,2,1,0:T(4,128)} %bitcast.3, s32[1,1,4]{2,1,0:T(1,128)} %slot_view_hbm.1), custom_call_target="tpu_custom_call" | custom-call | tf_op jit(solution)/shard_map/pallas_call | solution.py:608
  29.8 0.8 %copy.6 = f32[32,32,32]{2,1,0:T(8,128)} copy(f32[32,32,32]{2,1,0:T(8,128)S(1)} %shard_map.46) | data formatting | bytes 262144

commit v4 on v2

--- a/solution.py
+++ b/solution.py
@@ -112,7 +112,7 @@
     for i in range(2 * RANK):
         done = dot(order, jnp.concatenate([m[i * 32 : i * 32 + 32] for m in wide], axis=0)).astype(BF16)
         if i < RANK:
-            ty[i] = done
+            ty[:, i * 256 : (i + 1) * 256] = done
         else:
             tyb[(i - RANK) * 128 : (i - RANK + 1) * 128, :] = done
 
@@ -300,19 +300,20 @@
     def swapped(jy, jx):
         core_copy(jy, jx, 1 - core).wait_recv()
 
-    def forward_z(jy, jx):
-        rows = slice(jx * 128, jx * 128 + 128)
-        rim = field[jy, jx, :, 8:10].reshape(256, LANES)
+    def forward_z(*blocks):
+        pieces = [(*b, side) for b in blocks for side in range(2)]
+        rim = jnp.concatenate([field[jy, jx, side, 8 + tp] for jy, jx, side in pieces for tp in range(2)])
         for g in range(GROUPS):
             turned = pltpu.roll(rim, LANES - 32 * g, 1) if g else rim
             main = jnp.concatenate(
-                [field[jy, jx, side, 4 * tp + g] for side in range(2) for tp in range(2)], axis=0
+                [field[jy, jx, side, 4 * tp + g] for jy, jx, side in pieces for tp in range(2)]
             )
             done = dot(jnp.concatenate([main, turned], axis=1), wz[...]).astype(BF16)
-            for r in range(RANK):
-                after_z[r, jy * GROUPS + g, :, rows, :] = done[:, r * 128 : (r + 1) * 128].reshape(
-                    2, 128, LANES
-                )
+            for i, (jy, jx, side) in enumerate(pieces):
+                for r in range(RANK):
+                    after_z[r, jy * GROUPS + g, side, jx * 128 : jx * 128 + 128, :] = done[
+                        i * 128 : (i + 1) * 128, r * 128 : (r + 1) * 128
+                    ]
 
     def forward_x(jy):
         for r in range(RANK):
@@ -365,7 +366,7 @@
 
     lax.fori_loop(0, 16, order_tile, 0, unroll=4)
     swapped(1, 1)
-    forward_z(1, 1)
+    forward_z((1, 1))
     for side in (0, 2):
         came(side, 1, 2, "u")
     for one, other in ((0, 2), (2, 0)):
@@ -380,9 +381,8 @@
     for side in (0, 2):
         swapped(1, side)
         swapped(side, 1)
-    for side in (0, 2):
-        forward_z(1, side)
-        forward_z(side, 1)
+    forward_z((1, 0), (1, 2))
+    forward_z((0, 1), (2, 1))
     waves = (((0, 0), (2, 2)), ((0, 2), (2, 0)))
     for corner in waves[0]:
         came(*corner, 0, "v")
@@ -398,22 +398,21 @@
     for wave in waves:
         for corner in wave:
             swapped(*corner)
-        for corner in wave:
-            forward_z(*corner)
+        forward_z(*wave)
     for jy in (0, 2):
         forward_x(jy)
 
     def along_y(step):
         quotient = []
         for b in range(2):
-            blurred = None
+            terms = []
             for r in range(RANK):
                 quads = [
                     after_x[r, 4 * b : 4 * b + 8, :, 16 * i : 16 * i + 16, :].reshape(256, LANES)
                     for i in range(4 * step, 4 * step + 4)
                 ]
-                part = dot(ty[r], jnp.concatenate(quads, axis=1))
-                blurred = part if blurred is None else blurred + part
+                terms.append(jnp.concatenate(quads, axis=1))
+            blurred = dot(ty[...], jnp.concatenate(terms, axis=0))
             rows = slice(128 * b, 128 * b + 128)
             quads = [seen[i, rows, :] for i in range(4 * step, 4 * step + 4)]
             quads = jnp.concatenate(quads, axis=1).astype(F32)
@@ -585,7 +584,7 @@
         pltpu.VMEM((VIEWS, 2, 64, LANES), F32),
         pltpu.VMEM((2, 24, LANES), F32),
         pltpu.VMEM((RANK, 128, 256), BF16),
-        pltpu.VMEM((RANK, 128, 256), BF16),
+        pltpu.VMEM((128, RANK * 256), BF16),
         pltpu.VMEM((256, RANK * LANES), BF16),
         pltpu.VMEM((RANK * 128, 256), BF16),
         pltpu.VMEM((2, RANK, 64, 256), BF16),

time: 30.7 us -> 30.7 us (level)
  no operation moved by 1% of the time
where the time goes in v4:
time: 30.7 us; the launch traced here: 30.4 us
  Pallas kernels  29.6 us (96%)
  local copies, waits for them, and re-layouts  0.8 us (3%)
    pallas_call x1, Pallas kernels, local(): pl.pallas_call(kernel, out_shape=pltpu.VMEM(estimate.shape, F32), in_spec...  29.6 us
    unnamed x1, local copies, waits for them, and re-layouts  0.8 us

profile of v4, /device:TPU:99, one launch (start us, length us, event | category | flops | bytes accessed | tf_op | source)
XLA Modules:
  0.0 30.4 jit_solution(18169136351367082798)
XLA Ops:
  0.0 29.6 %shard_map.46 = f32[32,32,32]{2,1,0:T(8,128)S(1)} custom-call(f32[32,32,32]{2,1,0:T(8,128)} %est_hbm.1, bf16[64,64,128]{2,1,0:T(8,128)(2,1)} %bitcast.2, f32[3,3,4,33]{3,2,1,0:T(4,128)} %bitcast.3, s32[1,1,4]{2,1,0:T(1,128)} %slot_view_hbm.1), custom_call_target="tpu_custom_call" | custom-call | tf_op jit(solution)/shard_map/pallas_call | solution.py:603
  29.6 0.8 %copy.6 = f32[32,32,32]{2,1,0:T(8,128)} copy(f32[32,32,32]{2,1,0:T(8,128)S(1)} %shard_map.46) | data formatting | bytes 262144

commit v5 on v4

--- a/solution.py
+++ b/solution.py
@@ -120,7 +120,7 @@
 def kernel(
     est_hbm, tile_hbm, psf_hbm, slot_view_hbm, refined,
     est, tile, psf, slot_view,
-    packed, parts, outer, field, after_z, after_x, seen, back_y, back_x, sums, rims,
+    packed, parts, outer, field, after_z, after_x, seen, quotient, back_y, back_x, sums, rims,
     got_core, got_chip, got_edge,
     taps, tx, ty, wz, tyb, txb, wb,
     load_sem, part_send, part_recv, face_send, face_recv, core_send, core_recv, sum_send, sum_recv, ready,
@@ -315,17 +315,39 @@
                         i * 128 : (i + 1) * 128, r * 128 : (r + 1) * 128
                     ]
 
-    def forward_x(jy):
+    def forward_x(jy, b):
         for r in range(RANK):
             for group in (jy * GROUPS, jy * GROUPS + 2):
-                for b in range(2):
-                    rows = slice(b * 128, b * 128 + 256)
-                    both = [after_z[r, group + k // 2, k % 2, rows, :] for k in range(4)]
-                    done = dot(tx[r], jnp.concatenate(both, axis=1)).astype(BF16)
-                    for k in range(4):
-                        after_x[r, group + k // 2, k % 2, b * 128 : b * 128 + 128, :] = done[
-                            :, k * 128 : k * 128 + 128
-                        ]
+                rows = slice(b * 128, b * 128 + 256)
+                both = [after_z[r, group + k // 2, k % 2, rows, :] for k in range(4)]
+                done = dot(tx[r], jnp.concatenate(both, axis=1)).astype(BF16)
+                for k in range(4):
+                    after_x[r, group + k // 2, k % 2, b * 128 : b * 128 + 128, :] = done[
+                        :, k * 128 : k * 128 + 128
+                    ]
+
+    def forward_y(step, b):
+        terms = []
+        for r in range(RANK):
+            quads = [
+                after_x[r, 4 * b : 4 * b + 8, :, 16 * i : 16 * i + 16, :].reshape(256, LANES)
+                for i in range(4 * step, 4 * step + 4)
+            ]
+            terms.append(jnp.concatenate(quads, axis=1))
+        blurred = dot(ty[...], jnp.concatenate(terms, axis=0))
+        rows = slice(128 * b, 128 * b + 128)
+        quads = [seen[i, rows, :] for i in range(4 * step, 4 * step + 4)]
+        quads = jnp.concatenate(quads, axis=1).astype(F32)
+        quotient[step, rows, :] = (RANK * quads / (blurred + RANK * BACKGROUND)).astype(BF16)
+
+    def backward_y(step):
+        for r in range(RANK):
+            done = dot(tyb[r * 128 : r * 128 + 128, :], quotient[step]).astype(BF16)
+            for k in range(4):
+                i = 4 * step + k
+                back_y[r * 8 : r * 8 + 8, 16 * i : 16 * i + 16, :] = done[
+                    :, k * 128 : k * 128 + 128
+                ].reshape(8, 16, LANES)
 
     assemble()
     for name in ("u_up", "u_down", "v_up", "v_down"):
@@ -384,47 +406,31 @@
     forward_z((1, 0), (1, 2))
     forward_z((0, 1), (2, 1))
     waves = (((0, 0), (2, 2)), ((0, 2), (2, 0)))
+
+    def wave_came(wave):
+        for corner in wave:
+            came(*corner, 0, "v")
+            came(*corner, 1, "u")
+            came(*corner, 2, "v")
+            pass_on(*corner)
+
+    wave_came(waves[0])
+    forward_x(1, 0)
+    forward_x(1, 1)
     for corner in waves[0]:
-        came(*corner, 0, "v")
-        came(*corner, 1, "u")
-        came(*corner, 2, "v")
-        pass_on(*corner)
-    forward_x(1)
+        swapped(*corner)
+    forward_z(*waves[0])
+    forward_x(0, 0)
+    forward_x(2, 1)
+    wave_came(waves[1])
+    for step in range(2):
+        forward_y(step, 0)
+        forward_y(step + 2, 1)
     for corner in waves[1]:
-        came(*corner, 0, "v")
-        came(*corner, 1, "u")
-        came(*corner, 2, "v")
-        pass_on(*corner)
-    for wave in waves:
-        for corner in wave:
-            swapped(*corner)
-        forward_z(*wave)
-    for jy in (0, 2):
-        forward_x(jy)
-
-    def along_y(step):
-        quotient = []
-        for b in range(2):
-            terms = []
-            for r in range(RANK):
-                quads = [
-                    after_x[r, 4 * b : 4 * b + 8, :, 16 * i : 16 * i + 16, :].reshape(256, LANES)
-                    for i in range(4 * step, 4 * step + 4)
-                ]
-                terms.append(jnp.concatenate(quads, axis=1))
-            blurred = dot(ty[...], jnp.concatenate(terms, axis=0))
-            rows = slice(128 * b, 128 * b + 128)
-            quads = [seen[i, rows, :] for i in range(4 * step, 4 * step + 4)]
-            quads = jnp.concatenate(quads, axis=1).astype(F32)
-            quotient.append((RANK * quads / (blurred + RANK * BACKGROUND)).astype(BF16))
-        quotient = jnp.concatenate(quotient, axis=0)
-        for r in range(RANK):
-            done = dot(tyb[r * 128 : r * 128 + 128, :], quotient).astype(BF16)
-            for k in range(4):
-                i = 4 * step + k
-                back_y[r * 8 : r * 8 + 8, 16 * i : 16 * i + 16, :] = done[
-                    :, k * 128 : k * 128 + 128
-                ].reshape(8, 16, LANES)
+        swapped(*corner)
+    forward_z(*waves[1])
+    forward_x(2, 0)
+    forward_x(0, 1)
 
     def backward_x(half):
         within = slice(half * 64, half * 64 + 192)
@@ -495,9 +501,11 @@
 
     pl.when(~last & above)(lambda: pl.semaphore_wait(ready, 1))
     for step in range(3):
-        along_y(step)
+        forward_y(step, 1 if step < 2 else 0)
+        backward_y(step)
     backward(0)
-    along_y(3)
+    forward_y(3, 0)
+    backward_y(3)
     pass_over(0)
     backward(1)
     pass_over(1)
@@ -575,6 +583,7 @@
         pltpu.VMEM((RANK, 12, 2, 384, LANES), BF16),
         pltpu.VMEM((RANK, 12, 2, 256, LANES), BF16),
         pltpu.VMEM((16, 256, LANES), BF16),
+        pltpu.VMEM((4, 256, 4 * LANES), BF16),
         pltpu.VMEM((24, 256, LANES), BF16),
         pltpu.VMEM((GROUPS, 2, 128, RANK * LANES), BF16),
         pltpu.VMEM((2, 4, 128, LANES), F32),

time: 30.7 us -> 31.9 us (1.039)
  Pallas kernels: 29.6 us -> 31 us
    pallas_call x1, Pallas kernels: 29.6 us -> 31 us  [local(): pl.pallas_call(kernel, out_shape=pltpu.VMEM(estimate.shape, F32), in_spec...]
where the time goes in v5:
time: 31.9 us; the launch traced here: 31.8 us
  Pallas kernels  31 us (97%)
  local copies, waits for them, and re-layouts  0.8 us (3%)
    pallas_call x1, Pallas kernels, local(): pl.pallas_call(kernel, out_shape=pltpu.VMEM(estimate.shape, F32), in_spec...  31 us
    unnamed x1, local copies, waits for them, and re-layouts  0.8 us

profile of v5, /device:TPU:99, one launch (start us, length us, event | category | flops | bytes accessed | tf_op | source)
XLA Modules:
  0.0 31.8 jit_solution(4325883223724357676)
XLA Ops:
  0.0 31.0 %shard_map.46 = f32[32,32,32]{2,1,0:T(8,128)S(1)} custom-call(f32[32,32,32]{2,1,0:T(8,128)} %est_hbm.1, bf16[64,64,128]{2,1,0:T(8,128)(2,1)} %bitcast.2, f32[3,3,4,33]{3,2,1,0:T(4,128)} %bitcast.3, s32[1,1,4]{2,1,0:T(1,128)} %slot_view_hbm.1), custom_call_target="tpu_custom_call" | custom-call | tf_op jit(solution)/shard_map/pallas_call | solution.py:612
  31.1 0.8 %copy.6 = f32[32,32,32]{2,1,0:T(8,128)} copy(f32[32,32,32]{2,1,0:T(8,128)S(1)} %shard_map.46) | data formatting | bytes 262144

commit v6 on v4

--- a/solution.py
+++ b/solution.py
@@ -483,7 +483,6 @@
             ).wait_recv()
 
     def backward(h):
-        backward_x(h)
         backward_z(h)
         far_swap[h].start()
         near_swap[h].start()
@@ -494,10 +493,11 @@
         over[h].start()
 
     pl.when(~last & above)(lambda: pl.semaphore_wait(ready, 1))
-    for step in range(3):
+    for step in range(4):
         along_y(step)
+    backward_x(0)
     backward(0)
-    along_y(3)
+    backward_x(1)
     pass_over(0)
     backward(1)
     pass_over(1)

time: 30.7 us -> 30.8 us (level)
  no operation moved by 1% of the time
where the time goes in v6:
time: 30.8 us; the launch traced here: 30.6 us
  Pallas kernels  29.8 us (97%)
  local copies, waits for them, and re-layouts  0.8 us (3%)
    pallas_call x1, Pallas kernels, local(): pl.pallas_call(kernel, out_shape=pltpu.VMEM(estimate.shape, F32), in_spec...  29.8 us
    unnamed x1, local copies, waits for them, and re-layouts  0.8 us

profile of v6, /device:TPU:99, one launch (start us, length us, event | category | flops | bytes accessed | tf_op | source)
XLA Modules:
  0.0 30.6 jit_solution(2280466872179705286)
XLA Ops:
  0.0 29.8 %shard_map.46 = f32[32,32,32]{2,1,0:T(8,128)S(1)} custom-call(f32[32,32,32]{2,1,0:T(8,128)} %est_hbm.1, bf16[64,64,128]{2,1,0:T(8,128)(2,1)} %bitcast.2, f32[3,3,4,33]{3,2,1,0:T(4,128)} %bitcast.3, s32[1,1,4]{2,1,0:T(1,128)} %slot_view_hbm.1), custom_call_target="tpu_custom_call" | custom-call | tf_op jit(solution)/shard_map/pallas_call | solution.py:603
  29.8 0.8 %copy.6 = f32[32,32,32]{2,1,0:T(8,128)} copy(f32[32,32,32]{2,1,0:T(8,128)S(1)} %shard_map.46) | data formatting | bytes 262144

commit v7 on v4

--- a/solution.py
+++ b/solution.py
@@ -236,7 +236,6 @@
     loads[1].wait()
     loads[2].wait()
     build_taps(psf, slot_view, slot, taps)
-    build_z(taps, wz, wb)
 
     def assemble():
         for k in range(1, VIEWS):
@@ -339,11 +338,12 @@
         for k in range(VIEWS):
             outer_copy(0, k, at_vert(vert + 1 + k), k % 2).start()
 
-    build_x(taps, bx, tx, txb)
+    build_z(taps, wz, wb)
     assemble_rims()
     for name in ("u_up", "u_down", "v_up", "v_down"):
         send_own(name, 2)
     pass_on(1, 1)
+    build_x(taps, bx, tx, txb)
     for side in (0, 2):
         came(side, 1, 0, "u")
     for one, other in ((0, 2), (2, 0)):

time: 30.7 us -> 30.7 us (level)
  no operation moved by 1% of the time
where the time goes in v7:
time: 30.7 us; the launch traced here: 30.4 us
  Pallas kernels  29.6 us (96%)
  local copies, waits for them, and re-layouts  0.8 us (3%)
    pallas_call x1, Pallas kernels, local(): pl.pallas_call(kernel, out_shape=pltpu.VMEM(estimate.shape, F32), in_spec...  29.6 us
    unnamed x1, local copies, waits for them, and re-layouts  0.8 us

profile of v7, /device:TPU:99, one launch (start us, length us, event | category | flops | bytes accessed | tf_op | source)
XLA Modules:
  0.0 30.4 jit_solution(7483042500443400466)
XLA Ops:
  0.0 29.6 %shard_map.46 = f32[32,32,32]{2,1,0:T(8,128)S(1)} custom-call(f32[32,32,32]{2,1,0:T(8,128)} %est_hbm.1, bf16[64,64,128]{2,1,0:T(8,128)(2,1)} %bitcast.2, f32[3,3,4,33]{3,2,1,0:T(4,128)} %bitcast.3, s32[1,1,4]{2,1,0:T(1,128)} %slot_view_hbm.1), custom_call_target="tpu_custom_call" | custom-call | tf_op jit(solution)/shard_map/pallas_call | solution.py:603
  29.6 0.8 %copy.6 = f32[32,32,32]{2,1,0:T(8,128)} copy(f32[32,32,32]{2,1,0:T(8,128)S(1)} %shard_map.46) | data formatting | bytes 262144

commit v8 on v4

--- a/solution.py
+++ b/solution.py
@@ -328,10 +328,10 @@
                         ]
 
     assemble()
-    for name in ("u_up", "u_down", "v_up", "v_down"):
-        send_own(name, 0)
-    for name in ("v_up", "v_down", "u_up", "u_down"):
-        send_own(name, 1)
+    for name, which in (("u_up", 0), ("u_down", 0), ("v_up", 1), ("v_down", 1)):
+        send_own(name, which)
+    for name, which in (("u_up", 1), ("u_down", 1), ("v_up", 0), ("v_down", 0)):
+        send_own(name, which)
 
     @pl.when(last & above)
     def _():

time: 30.7 us -> 30.5 us (level)
  no operation moved by 1% of the time
where the time goes in v8:
time: 30.5 us; the launch traced here: 30.3 us
  Pallas kernels  29.5 us (97%)
  local copies, waits for them, and re-layouts  0.8 us (3%)
    pallas_call x1, Pallas kernels, local(): pl.pallas_call(kernel, out_shape=pltpu.VMEM(estimate.shape, F32), in_spec...  29.5 us
    unnamed x1, local copies, waits for them, and re-layouts  0.8 us

profile of v8, /device:TPU:99, one launch (start us, length us, event | category | flops | bytes accessed | tf_op | source)
XLA Modules:
  0.0 30.3 jit_solution(9921317002181398396)
XLA Ops:
  0.0 29.5 %shard_map.46 = f32[32,32,32]{2,1,0:T(8,128)S(1)} custom-call(f32[32,32,32]{2,1,0:T(8,128)} %est_hbm.1, bf16[64,64,128]{2,1,0:T(8,128)(2,1)} %bitcast.2, f32[3,3,4,33]{3,2,1,0:T(4,128)} %bitcast.3, s32[1,1,4]{2,1,0:T(1,128)} %slot_view_hbm.1), custom_call_target="tpu_custom_call" | custom-call | tf_op jit(solution)/shard_map/pallas_call | solution.py:603
  29.5 0.8 %copy.6 = f32[32,32,32]{2,1,0:T(8,128)} copy(f32[32,32,32]{2,1,0:T(8,128)S(1)} %shard_map.46) | data formatting | bytes 262144

commit v9 on v8

--- a/solution.py
+++ b/solution.py
@@ -395,9 +395,9 @@
         came(*corner, 1, "u")
         came(*corner, 2, "v")
         pass_on(*corner)
+    for corner in waves[0] + waves[1]:
+        swapped(*corner)
     for wave in waves:
-        for corner in wave:
-            swapped(*corner)
         forward_z(*wave)
     for jy in (0, 2):
         forward_x(jy)

time: 30.5 us -> 30.8 us (level)
  no operation moved by 1% of the time
where the time goes in v9:
time: 30.8 us; the launch traced here: 30.6 us
  Pallas kernels  29.8 us (97%)
  local copies, waits for them, and re-layouts  0.8 us (3%)
    pallas_call x1, Pallas kernels, local(): pl.pallas_call(kernel, out_shape=pltpu.VMEM(estimate.shape, F32), in_spec...  29.8 us
    unnamed x1, local copies, waits for them, and re-layouts  0.8 us

profile of v9, /device:TPU:99, one launch (start us, length us, event | category | flops | bytes accessed | tf_op | source)
XLA Modules:
  0.0 30.6 jit_solution(15055775522667014614)
XLA Ops:
  0.0 29.8 %shard_map.46 = f32[32,32,32]{2,1,0:T(8,128)S(1)} custom-call(f32[32,32,32]{2,1,0:T(8,128)} %est_hbm.1, bf16[64,64,128]{2,1,0:T(8,128)(2,1)} %bitcast.2, f32[3,3,4,33]{3,2,1,0:T(4,128)} %bitcast.3, s32[1,1,4]{2,1,0:T(1,128)} %slot_view_hbm.1), custom_call_target="tpu_custom_call" | custom-call | tf_op jit(solution)/shard_map/pallas_call | solution.py:603
  29.8 0.8 %copy.6 = f32[32,32,32]{2,1,0:T(8,128)} copy(f32[32,32,32]{2,1,0:T(8,128)S(1)} %shard_map.46) | data formatting | bytes 262144
